TPU v7x, 32 devices: a whole 2x2x4 slice. The times are simulated.
32 devices in a mesh: amp: 32 (over z, y, x, core).
Axes of the slice: x: 2, y: 2, z: 4, core: 2. Of those that a mesh axis runs over, the one named last changes fastest.
Arguments:
- state: float32 [2, 4194304], P(None, 'amp'), may hold values from -6 to 6
- costate: float32 [2, 4194304], P(None, 'amp'), may hold values from -6 to 6
- gates: float32 [3, 2, 128, 128], replicated, may hold values from -1 to 1, as said below
Outputs:
- state_out: float32 [2, 4194304], P(None, 'amp')
- costate_out: float32 [2, 4194304], P(None, 'amp')
- gradients: float32 [3, 2, 128, 128], replicated
Inputs may be any that keep to these rules, and one draw needn't show every extreme that they name: Each gates[l, 0] + i gates[l, 1] is a unitary matrix.
All inputs are finite; a program needn't handle non-finite values.
Results may differ from a plain program's by a relative error of at most 0.0001.
Values sent between devices are 32-bit elements; how exact they have to be, the bound alone decides.
No kernel may reach another device: no remote copies, remote signals or barrier semaphores. Data moves between devices by JAX's collectives and lax.ppermute only.
A program may use at most 64 MiB of HBM per device.

v0:
```python
import functools
import math

import jax
import jax.numpy as jnp
from jax import lax
from jax.experimental import pallas as pl
from jax.experimental.pallas import tpu as pltpu
from jax.sharding import PartitionSpec as P

VMEM_BYTES = 12 * 1024 * 1024


def split(value):
    high = value.astype(jnp.bfloat16)
    low = (value - high.astype(jnp.float32)).astype(jnp.bfloat16)
    return high, low


def both_parts(value):
    return jnp.concatenate(split(value), axis=0)


def left_parts(both):
    rows = both.shape[0] // 2
    high, low = both[:rows], both[rows:]
    return jnp.concatenate([high, low, high], axis=1)


def dot_parts(left, right):
    high, low = split(right)
    return jnp.dot(
        left_parts(left),
        jnp.concatenate([high, high, low], axis=0),
        preferred_element_type=jnp.float32,
    )


def dot_parts_rows(left, right):
    high, low = split(right)
    return lax.dot_general(
        left_parts(left),
        jnp.concatenate([high, high, low], axis=1),
        (((1,), (1,)), ((), ())),
        preferred_element_type=jnp.float32,
    )


def lane_index(shape):
    return lax.broadcasted_iota(jnp.int32, shape, len(shape) - 1)


def swap_groups(values):
    lanes = values[0].shape[-1]
    group = lane_index(values[0].shape) // (lanes // 4)
    for bit in (2, 1):
        width = bit * (lanes // 4)
        fresh = list(values)
        for index in range(4):
            if index & bit == 0:
                low, high = values[index], values[index | bit]
                upper = group & bit != 0
                fresh[index] = jnp.where(upper, pltpu.roll(high, width, 1), low)
                fresh[index | bit] = jnp.where(upper, high, pltpu.roll(low, lanes - width, 1))
        values = fresh
    return values


def swap_bit(low, high):
    lanes = low.shape[-1]
    width = lanes // 4
    upper = (lane_index(low.shape) // width) % 2 == 1
    first = jnp.where(upper, pltpu.roll(high, width, 1), low)
    second = jnp.where(upper, high, pltpu.roll(low, lanes - width, 1))
    return first, second


def row_halves(value, groups):
    rows, lanes = value.shape
    parts = value.reshape(groups, 2, rows // groups // 2, lanes)
    return parts[:, 0].reshape(rows // 2, lanes), parts[:, 1].reshape(rows // 2, lanes)


def wait_all(copies):
    for copy in copies:
        copy.wait()


def undo_matrix(gate):
    real, imag = gate[0].T, gate[1].T
    top = jnp.concatenate([real, imag], axis=1)
    low = jnp.concatenate([-imag, real], axis=1)
    return both_parts(jnp.concatenate([top, low], axis=0))


def column(rows, block, order):
    stride = rows.shape[0] // order
    parts = [rows[pl.ds(block * 2 + part, order, stride=stride), :] for part in range(2)]
    return jnp.concatenate(parts, axis=0)


def first_kernel(
    state_ref, costate_ref, gates_ref, out_ref, gate, rows, field_ref, gate_sem, row_sems, out_sems
):
    order = gate.shape[1]
    lanes = rows.shape[2]
    stride = rows.shape[1] // order
    chunks = row_sems.shape[1]
    chunk = rows.shape[1] // chunks
    copies = [pltpu.make_async_copy(gates_ref.at[0], gate, gate_sem)]
    for index in range(chunks):
        part = pl.ds(index * chunk, chunk)
        for vector, ref in enumerate((state_ref, costate_ref)):
            copies.append(
                pltpu.make_async_copy(ref.at[part], rows.at[vector, part], row_sems.at[vector, index])
            )
    for copy in copies:
        copy.start()
    copies[0].wait()
    matrix = undo_matrix(gate)
    wait_all(copies[1:])

    def column(vector, block):
        parts = [rows[vector, pl.ds(block * 2 + part, order, stride=stride), :] for part in range(2)]
        return jnp.concatenate(parts, axis=0)

    out_copies = []
    for block in range(stride // 2):
        field = jnp.concatenate([column(0, block), column(1, block)], axis=1)
        undone = dot_parts(matrix, field)
        pieces = []
        for vector in range(2):
            pieces += row_halves(undone[:, vector * lanes : (vector + 1) * lanes], 2)
        for index, piece in enumerate(swap_groups(pieces)):
            field_ref[block * 4 + index] = piece
        part = pl.ds(block * 4, 4)
        copy = pltpu.make_async_copy(field_ref.at[part], out_ref.at[part], out_sems.at[block])
        copy.start()
        out_copies.append(copy)
    wait_all(out_copies)


def outer_product(lam, psi):
    order = lam.shape[0] // 2
    left = jnp.concatenate([lam[:order], lam[order:]], axis=1)
    plain = jnp.concatenate([psi[:order], psi[order:]], axis=1)
    other = jnp.concatenate([-psi[order:], psi[:order]], axis=1)
    return dot_parts_rows(both_parts(left), jnp.concatenate([plain, other], axis=0))


def four_products(fields, groups):
    pieces = swap_groups(fields)
    rows, lanes = pieces[0].shape

    def joined(vector):
        parts = [
            piece.reshape(groups, 1, rows // groups, lanes)
            for piece in pieces[2 * vector : 2 * vector + 2]
        ]
        return jnp.concatenate(parts, axis=1).reshape(2 * rows, lanes)

    return outer_product(joined(1), joined(0))


def early_kernel(state_ref, costate_ref, out_ref):
    order = out_ref.shape[0]
    out_ref[...] = jnp.zeros_like(out_ref)

    @pl.loop(0, state_ref.shape[0] // order // 2)
    def _(block):
        out_ref[...] += outer_product(
            column(costate_ref, block, order), column(state_ref, block, order)
        )


def middle_kernel(moved_ref, gates_ref, out_ref, kept, last, sems):
    _, steps, _, order, lanes = moved_ref.shape
    batches = 2 * steps
    copies = []

    def undo(matrix, fields):
        result = dot_parts(matrix, jnp.concatenate(fields, axis=1))
        return [result[:, index * lanes : (index + 1) * lanes] for index in range(len(fields))]

    matrices = [undo_matrix(gates_ref[index + 1]) for index in range(2)]
    for step in range(steps):
        fields = [mixed_rows(moved_ref, step, bit) for bit in range(2)]
        for bit, result in enumerate(undo(matrices[0], fields)):
            for top, piece in enumerate(swap_bit(*row_halves(result, 8))):
                place = (top * steps + step) * 2 + bit
                kept[pl.ds(place * order, order), :] = piece

    for step in range(steps):
        fields = [regrouped(kept, step * 2 + index, order) for index in range(2)]
        for index, result in enumerate(undo(matrices[1], fields)):
            for bit, piece in enumerate(swap_bit(*row_halves(result, 2))):
                last[bit * batches + step * 2 + index] = piece
        for bit in range(2):
            part = pl.ds(bit * batches + step * 2, 2)
            copy = pltpu.make_async_copy(last.at[part], out_ref.at[part], sems.at[bit, step])
            copy.start()
            copies.append(copy)
    wait_all(copies)


def regrouped(kept_ref, batch, order):
    devices = kept_ref.shape[0] // order
    parts = [
        kept_ref[pl.ds(row * (devices // 2) + batch, devices, stride=order), :] for row in range(8)
    ]
    return jnp.concatenate(parts, axis=0)


def mixed_rows(moved_ref, step, bit):
    low_rows = moved_ref.shape[3] // 4
    parts = [
        moved_ref[top, step, low, pl.ds((part * 2 + bit) * low_rows, low_rows), :]
        for part in range(2)
        for top in range(2)
        for low in range(2)
    ]
    return jnp.concatenate(parts, axis=0)


def late_kernel(moved_ref, last_ref, early_ref, gates_ref, out_ref, sum_ref, *, scale):
    order = early_ref.shape[0]
    steps = moved_ref.shape[1]
    sum_ref[0] = early_ref[...]
    sum_ref[1:3] = jnp.zeros((2,) + early_ref.shape, jnp.float32)

    @pl.loop(0, steps)
    def _(step):
        first, second = (mixed_rows(moved_ref, step, bit) for bit in range(2))
        half = first.shape[-1] // 2
        lower = lane_index(first.shape) < half
        psi = jnp.where(lower, first, pltpu.roll(second, half, 1))
        lam = jnp.where(lower, pltpu.roll(first, half, 1), second)
        sum_ref[1] += outer_product(lam, psi)
        sum_ref[2] += four_products([last_ref[step * 4 + index] for index in range(4)], 2)

    for index in range(3):
        total = (sum_ref[index, :, :order], sum_ref[index, :, order:])
        gate = (gates_ref[index, 0], gates_ref[index, 1])
        left, right = (gate, total) if index == 2 else (total, gate)
        out_ref[index, 0], out_ref[index, 1] = complex_product(left, right, scale)


def complex_product(left, right, scale):
    def times(first, second):
        return jnp.dot(
            first, second, precision=lax.Precision.HIGHEST, preferred_element_type=jnp.float32
        )

    real = times(left[0], right[0]) - times(left[1], right[1])
    imag = times(left[0], right[1]) + times(left[1], right[0])
    return real * scale, imag * scale


def last_kernel(moved_ref, state_ref, costate_ref, rows, copy_sems):
    half = moved_ref.shape[1] // 2
    copies = []
    for block in range(rows.shape[1] // 2):
        pieces = swap_groups([moved_ref[block * 4 + index] for index in range(4)])
        for vector, ref in enumerate((state_ref, costate_ref)):
            for part in range(2):
                column = block * 2 + part
                for bit in range(2):
                    piece = pieces[2 * vector + bit][part * half : (part + 1) * half]
                    rows[vector, column, bit * half : (bit + 1) * half] = piece
                copy = pltpu.make_async_copy(
                    rows.at[vector, column], ref.at[:, column, 0], copy_sems.at[vector, column]
                )
                copy.start()
                copies.append(copy)
    wait_all(copies)


def gather_kernel(*refs):
    *part_refs, out_ref, copy_sems = refs
    place = lax.rem(lax.axis_index("amp"), len(part_refs))
    copies = [
        pltpu.make_async_copy(ref, out_ref.at[place ^ index], copy_sems.at[index])
        for index, ref in enumerate(part_refs)
    ]
    for copy in copies:
        copy.start()
    wait_all(copies)


def tree_sum(parts):
    while len(parts) > 1:
        parts = [parts[i] + parts[i + 1] for i in range(0, len(parts), 2)]
    return parts[0]


def exchange(part, distance):
    devices = lax.axis_size("amp")
    return lax.ppermute(part, "amp", [(i, i ^ distance) for i in range(devices)])


def scattered_sum(value):
    devices = lax.axis_size("amp")
    inner = min(8, devices)
    own = lax.axis_index("amp") % inner
    blocks = value.reshape(inner, -1, value.shape[-1])

    def pick(index):
        return lax.dynamic_index_in_dim(blocks, index, 0, keepdims=False)

    part = tree_sum([pick(own)] + [exchange(pick(own ^ k), k) for k in range(1, inner)])
    distance = inner
    while distance < devices:
        part = part + exchange(part, distance)
        distance *= 2
    return part


def gathered_chips(part):
    inner = min(8, lax.axis_size("amp"))
    return [part] + [exchange(part, k) for k in range(2, inner, 2)]


def gathered_cores(own, shape):
    others = [exchange(found, 1) for found in own]
    parts = [found for pair in zip(own, others) for found in pair]
    out = pl.pallas_call(
        gather_kernel,
        in_specs=[pl.BlockSpec(memory_space=pl.ANY)] * len(parts),
        out_specs=IN_HBM,
        out_shape=jax.ShapeDtypeStruct((len(parts),) + parts[0].shape, parts[0].dtype),
        scratch_shapes=[pltpu.SemaphoreType.DMA((len(parts),))],
        compiler_params=PARAMS,
    )(*parts)
    return out.reshape(shape)


def to_rows(field, lanes):
    return field.reshape(2, -1, lanes).swapaxes(0, 1).reshape(-1, lanes)


def from_rows(rows):
    return rows.reshape(-1, 2, rows.shape[-1]).swapaxes(0, 1).reshape(2, -1)


IN_HBM = pl.BlockSpec(memory_space=pltpu.HBM)
IN_VMEM = pl.BlockSpec(memory_space=pltpu.VMEM)
PARAMS = pltpu.CompilerParams(vmem_limit_bytes=VMEM_BYTES)
HBM_PARAMS = pltpu.CompilerParams(vmem_limit_bytes=60 * 1024 * 1024)


def cost(layers, amplitudes, order):
    flops = layers * 3 * 8 * amplitudes * order
    return pl.CostEstimate(flops=flops, bytes_accessed=32 * amplitudes, transcendentals=0)


def on_device_lanes(state, costate, gates, devices, order, columns):
    lanes = 4 * columns // devices
    steps = devices // 4
    rows = 2 * columns // lanes
    scale = 1.0 / math.sqrt(devices * columns)
    field_shape = (devices, order, lanes)
    sum_shape = (order, 2 * order)
    amplitudes = 2 * order * columns

    def array(shape, kind=jnp.float32):
        return jax.ShapeDtypeStruct(shape, kind)

    state, costate = to_rows(state, lanes), to_rows(costate, lanes)
    sent = pl.pallas_call(
        first_kernel,
        in_specs=[IN_HBM, IN_HBM, IN_HBM],
        out_specs=IN_HBM,
        out_shape=array(field_shape),
        scratch_shapes=[
            pltpu.VMEM((2, order, order), jnp.float32),
            pltpu.VMEM((2, rows * order, lanes), jnp.float32),
            pltpu.VMEM(field_shape, jnp.float32),
            pltpu.SemaphoreType.DMA,
            pltpu.SemaphoreType.DMA((2, 4)),
            pltpu.SemaphoreType.DMA((steps,)),
        ],
        compiler_params=HBM_PARAMS,
        cost_estimate=cost(1, amplitudes, order),
    )(state, costate, gates)
    state, costate, sent = lax.optimization_barrier((state, costate, sent))
    moved = lax.all_to_all(sent, "amp", 0, 0, tiled=True)
    early = pl.pallas_call(
        early_kernel,
        in_specs=[IN_VMEM, IN_VMEM],
        out_specs=IN_VMEM,
        out_shape=array(sum_shape),
        compiler_params=PARAMS,
        cost_estimate=cost(1, amplitudes, order),
    )(state, costate)
    moved = moved.reshape(2, steps, 2, order, lanes)
    last = pl.pallas_call(
        middle_kernel,
        in_specs=[IN_VMEM, IN_VMEM],
        out_specs=IN_HBM,
        out_shape=pltpu.HBM(field_shape, jnp.float32),
        scratch_shapes=[
            pltpu.VMEM((devices * order, lanes), jnp.float32),
            pltpu.VMEM(field_shape, jnp.float32),
            pltpu.SemaphoreType.DMA((2, steps)),
        ],
        compiler_params=PARAMS,
        cost_estimate=cost(2, amplitudes, order),
    )(moved, gates)
    arrived = lax.all_to_all(last, "amp", 0, 0, tiled=True)
    gradients = pl.pallas_call(
        functools.partial(late_kernel, scale=scale),
        in_specs=[IN_VMEM, IN_VMEM, IN_VMEM, IN_VMEM],
        out_specs=IN_VMEM,
        out_shape=array(gates.shape),
        scratch_shapes=[pltpu.VMEM((3,) + sum_shape, jnp.float32)],
        compiler_params=PARAMS,
        cost_estimate=cost(2, amplitudes, order),
    )(moved, last, early, gates)
    part, arrived = lax.optimization_barrier((scattered_sum(gradients), arrived))
    parts = gathered_chips(part)
    state_rows, costate_rows = pl.pallas_call(
        last_kernel,
        in_specs=[IN_VMEM],
        out_specs=[IN_HBM, IN_HBM],
        out_shape=[array((order, rows, 1, lanes))] * 2,
        scratch_shapes=[
            pltpu.VMEM((2, rows, order, lanes), jnp.float32),
            pltpu.SemaphoreType.DMA((2, rows)),
        ],
        compiler_params=PARAMS,
        cost_estimate=cost(1, amplitudes, order),
    )(arrived)
    for index in range(1, len(parts)):
        parts[index], state_rows = lax.optimization_barrier((parts[index], state_rows))
    gradients = gathered_cores(parts, gates.shape)
    return from_rows(state_rows), from_rows(costate_rows), gradients


def undo_gate(field, gate):
    high = lax.Precision.HIGHEST
    shape = field.shape
    parts = field.reshape(shape[:-1] + (2, 2, -1))
    real, imag = parts[..., 0, :], parts[..., 1, :]

    def contract(matrix, operand):
        return jnp.einsum("ts,btvc->bsvc", matrix, operand, precision=high)

    new_real = contract(gate[0], real) + contract(gate[1], imag)
    new_imag = contract(gate[0], imag) - contract(gate[1], real)
    return jnp.stack([new_real, new_imag], axis=-2).reshape(shape)


def gate_gradient(before, after):
    high = lax.Precision.HIGHEST
    lam = before.reshape(before.shape[:-1] + (2, 2, -1))[..., 1, :, :]
    psi = after.reshape(after.shape[:-1] + (2, 2, -1))[..., 0, :, :]
    real = jnp.einsum("btpc,bspc->ts", lam, psi, precision=high)
    imag = jnp.einsum("btc,bsc->ts", lam[..., 1, :], psi[..., 0, :], precision=high) - jnp.einsum(
        "btc,bsc->ts", lam[..., 0, :], psi[..., 1, :], precision=high
    )
    return jnp.stack([real, imag], axis=0)


def on_device_plain(state, costate, gates, devices, order, columns):
    own = columns // devices
    both = jnp.stack([state, costate], axis=0).reshape(2, 2, order, devices, own)
    field = both.transpose(3, 2, 0, 1, 4).reshape(devices, order, 4 * own)
    field = lax.all_to_all(field, "amp", 0, 0, tiled=True)
    after = undo_gate(field, gates[0])
    terms = [gate_gradient(field, after)]
    field = after.reshape(2, devices // 4, 2, 2, 2, order // 4, 4 * own)
    field = field.transpose(3, 1, 4, 0, 2, 5, 6).reshape(devices, order, 4 * own)
    after = undo_gate(field, gates[1])
    terms.append(gate_gradient(field, after))
    field = after.reshape(devices, order // devices, devices, 4 * own)
    field = field.transpose(2, 1, 0, 3).reshape(devices, order, 4 * own)
    after = undo_gate(field, gates[2])
    terms.append(gate_gradient(field, after))
    terms = jnp.stack(terms, axis=0) / math.sqrt(devices * columns)
    gradients = gathered_cores(gathered_chips(scattered_sum(terms)), gates.shape)
    field = lax.all_to_all(after, "amp", 0, 0, tiled=True)
    field = field.reshape(devices, order, 2, 2, own).transpose(2, 3, 1, 0, 4)
    field = field.reshape(2, 2, order * columns)
    return field[0], field[1], gradients


def on_device(state, costate, gates):
    devices = lax.axis_size("amp")
    order = gates.shape[2]
    columns = state.shape[1] // order
    filled = 4 * columns == 128 * devices and order == 4 * devices
    form = on_device_lanes if filled else on_device_plain
    return form(state, costate, gates, devices, order, columns)


def solution(mesh):
    return jax.shard_map(
        on_device,
        mesh=mesh,
        in_specs=(P(None, "amp"), P(None, "amp"), P()),
        out_specs=(P(None, "amp"), P(None, "amp"), P()),
        check_vma=False,
    )
```

profile of v0, /device:TPU:0, one launch (start us, length us, event | category | flops | bytes accessed | tf_op | source)
XLA Modules:
  0.0 129.6 jit_solution(18038522036493155617)
XLA Ops:
  0.6 4.5 %shard_map.58 = f32[32,128,128]{2,1,0:T(8,128)} custom-call(f32[2048,128]{1,0:T(8,128)} %bitcast.45, f32[2048,128]{1,0:T(8,128)} %bitcast.47, f32[3,2,128,128]{3,2,1,0:T(8,128)} %gates_ref.5), custom_call_target="tpu_custom_call" | custom-call | flops 805306368 | bytes 8388608 | tf_op jit(solution)/shard_map/pallas_call | solution.py:369
  5.2 0.0 copy-start.5
  5.2 56.0 %all_to_all.10 = f32[32,128,128]{2,1,0:T(8,128)S(1)} all-to-all(f32[32,128,128]{2,1,0:T(8,128)} %shard_map.58), channel_id=1, replica_groups=mesh['amp'=32] {'amp'}, dimensions={0} | all-to-all | bytes 4194304 | tf_op jit(solution)/shard_map/all_to_all | solution.py:386
  61.2 0.0 copy-done.5
  61.2 4.1 %shard_map.59.last_ref = f32[32,128,128]{2,1,0:T(8,128)} custom-call(f32[2,8,2,128,128]{4,3,2,1,0:T(8,128)S(1)} %bitcast.43, f32[3,2,128,128]{3,2,1,0:T(8,128)S(1)} %copy-done.5), custom_call_target="tpu_custom_call" | custom-call | flops 1610612736 | bytes 8388608 | tf_op jit(solution)/shard_map/pallas_call | solution.py:396
  65.3 0.0 copy-start.3
  65.4 3.7 %all-to-all-start.1 = ((f32[32,128,128]{2,1,0:T(8,128)}), f32[32,128,128]{2,1,0:T(8,128)S(1)}, u32[]{:S(2)}, u32[]{:S(2)}) async-start(f32[32,128,128]{2,1,0:T(8,128)} %shard_map.59.last_ref), calls=%async_computation.1 | async-start | bytes 4194304 | tf_op jit(solution)/shard_map/all_to_all | solution.py:409
  69.1 0.0 copy-done.3
  69.1 0.0 copy-start.4
  69.1 1.2 copy-done.4
  70.3 2.4 %shard_map.60.early_ref = f32[128,256]{1,0:T(8,128)S(1)} custom-call(f32[2048,128]{1,0:T(8,128)S(1)} %bitcast.46, f32[2048,128]{1,0:T(8,128)S(1)} %bitcast.48), custom_call_target="tpu_custom_call" | custom-call | flops 805306368 | bytes 8388608 | tf_op jit(solution)/shard_map/pallas_call | solution.py:387
  72.7 1.6 %copy-done.2 = f32[32,128,128]{2,1,0:T(8,128)S(1)} copy-done((f32[32,128,128]{2,1,0:T(8,128)S(1)}, f32[32,128,128]{2,1,0:T(8,128)}, u32[]{:S(2)}) %copy-start.2) | copy-done | bytes 2097176
  74.3 5.8 %shard_map.61 = f32[3,2,128,128]{3,2,1,0:T(8,128)S(1)} custom-call(f32[2,8,2,128,128]{4,3,2,1,0:T(8,128)S(1)} %bitcast.44, f32[32,128,128]{2,1,0:T(8,128)S(1)} %copy-done, f32[128,256]{1,0:T(8,128)S(1)} %shard_map.60.early_ref, f32[3,2,128,128]{3,2,1,0:T(8,128)S(1)} %copy-done.5), custom_call_target="tpu_custom_call" | custom-call | flops 1610612736 | bytes 8388608 | tf_op jit(solution)/shard_map/pallas_call | solution.py:410
  80.2 0.3 collective-permute-start
  80.5 2.6 %collective-permute-start.5 = (f32[96,128]{1,0:T(8,128)S(1)}, f32[96,128]{1,0:T(8,128)S(1)}, u32[]{:S(2)}, u32[]{:S(2)}) collective-permute-start(f32[96,128]{1,0:T(8,128)S(1)} %get-tuple-element.31), channel_id=1, source_target_pairs={{0,6},{1,7},{2,4},{3,5},{4,2},{5,3},{6,0},{7,1},{8,14},{9,15},{10,... | collective-permute-start | bytes 147464 | tf_op jit(solution)/shard_map/ppermute | solution.py:298
  83.1 0.0 collective-permute-start.6
  83.1 1.7 %collective-permute-start.3 = (f32[96,128]{1,0:T(8,128)S(1)}, f32[96,128]{1,0:T(8,128)S(1)}, u32[]{:S(2)}, u32[]{:S(2)}) collective-permute-start(f32[96,128]{1,0:T(8,128)S(1)} %get-tuple-element.33), channel_id=1, source_target_pairs={{0,4},{1,5},{2,6},{3,7},{4,0},{5,1},{6,2},{7,3},{8,12},{9,13},{10,... | collective-permute-start | bytes 147464 | tf_op jit(solution)/shard_map/ppermute | solution.py:298
  84.8 0.1 collective-permute-start.4
  84.9 0.0 collective-permute-done
  84.9 1.7 %collective-permute-start.1 = (f32[96,128]{1,0:T(8,128)S(1)}, f32[96,128]{1,0:T(8,128)S(1)}, u32[]{:S(2)}, u32[]{:S(2)}) collective-permute-start(f32[96,128]{1,0:T(8,128)S(1)} %get-tuple-element.34), channel_id=1, source_target_pairs={{0,2},{1,3},{2,0},{3,1},{4,6},{5,7},{6,4},{7,5},{8,10},{9,11},{10,... | collective-permute-start | bytes 147464 | tf_op jit(solution)/shard_map/ppermute | solution.py:298
  86.6 0.0 collective-permute-done.5
  86.6 0.3 collective-permute-start.2
  86.9 1.7 %collective-permute-done.6 = f32[96,128]{1,0:T(8,128)S(1)} collective-permute-done((f32[96,128]{1,0:T(8,128)S(1)}, f32[96,128]{1,0:T(8,128)S(1)}, u32[]{:S(2)}, u32[]{:S(2)}) %collective-permute-start.6) | collective-permute-done | bytes 49184 | tf_op jit(solution)/shard_map/ppermute | solution.py:298
  88.6 3.2 %collective-permute-done.3 = f32[96,128]{1,0:T(8,128)S(1)} collective-permute-done((f32[96,128]{1,0:T(8,128)S(1)}, f32[96,128]{1,0:T(8,128)S(1)}, u32[]{:S(2)}, u32[]{:S(2)}) %collective-permute-start.3) | collective-permute-done | bytes 49184 | tf_op jit(solution)/shard_map/ppermute | solution.py:298
  91.7 1.8 %collective-permute-done.4 = f32[96,128]{1,0:T(8,128)S(1)} collective-permute-done((f32[96,128]{1,0:T(8,128)S(1)}, f32[96,128]{1,0:T(8,128)S(1)}, u32[]{:S(2)}, u32[]{:S(2)}) %collective-permute-start.4) | collective-permute-done | bytes 49184 | tf_op jit(solution)/shard_map/ppermute | solution.py:298
  93.5 0.0 collective-permute-done.1
  93.5 0.0 collective-permute-done.2
  93.5 0.1 collective-permute-start.7
  93.6 11.7 %collective-permute-done.7 = f32[96,128]{1,0:T(8,128)S(1)} collective-permute-done((f32[96,128]{1,0:T(8,128)S(1)}, f32[96,128]{1,0:T(8,128)S(1)}, u32[]{:S(2)}, u32[]{:S(2)}) %collective-permute-start.7) | collective-permute-done | bytes 49184 | tf_op jit(solution)/shard_map/ppermute | solution.py:298
  105.3 4.1 %collective-permute-start.8 = (f32[96,128]{1,0:T(8,128)S(1)}, f32[96,128]{1,0:T(8,128)S(1)}, u32[]{:S(2)}, u32[]{:S(2)}) collective-permute-start(f32[96,128]{1,0:T(8,128)S(1)} %add.72), channel_id=1, source_target_pairs={{0,16},{1,17},{2,18},{3,19},{4,20},{5,21},{6,22},{7,23},{8,24},{9,... | collective-permute-start | bytes 147464 | tf_op jit(solution)/shard_map/ppermute | solution.py:298
  109.4 10.6 %collective-permute-done.8 = f32[96,128]{1,0:T(8,128)S(1)} collective-permute-done((f32[96,128]{1,0:T(8,128)S(1)}, f32[96,128]{1,0:T(8,128)S(1)}, u32[]{:S(2)}, u32[]{:S(2)}) %collective-permute-start.8) | collective-permute-done | bytes 49184 | tf_op jit(solution)/shard_map/ppermute | solution.py:298
  120.0 0.0 all-to-all-done.1.moved_ref
  120.0 2.4 %collective-permute-start.9 = (f32[96,128]{1,0:T(8,128)S(1)}, f32[96,128]{1,0:T(8,128)S(1)}, u32[]{:S(2)}, u32[]{:S(2)}) collective-permute-start(f32[96,128]{1,0:T(8,128)S(1)} %add.73.refs_0_), channel_id=1, source_target_pairs={{0,6},{1,7},{2,4},{3,5},{4,2},{5,3},{6,0},{7,1},{8,14},{9,15},{10,... | collective-permute-start | bytes 147464 | tf_op jit(solution)/shard_map/ppermute | solution.py:298
  122.3 0.6 collective-permute-start.10
  123.0 0.6 collective-permute-start.11
  123.5 0.0 collective-permute-start.12
  123.5 2.4 %shard_map.62 = (f32[128,16,1,128]{3,2,1,0:T(1,128)}, f32[128,16,1,128]{3,2,1,0:T(1,128)}) custom-call(f32[32,128,128]{2,1,0:T(8,128)S(1)} %all-to-all-done.1.moved_ref), custom_call_target="tpu_custom_call" | custom-call | flops 805306368 | bytes 8388608 | tf_op jit(solution)/shard_map/pallas_call | solution.py:421
  125.9 1.2 collective-permute-done.11.refs_2_
  127.1 0.0 collective-permute-done.10.refs_4_
  127.1 0.0 collective-permute-done.9.refs_6_
  127.1 0.0 collective-permute-start.13
  127.1 0.5 collective-permute-start.14
  127.6 0.1 collective-permute-start.15
  127.6 0.0 collective-permute-done.12.refs_1_
  127.7 0.6 collective-permute-done.13.refs_3_
  128.3 0.2 collective-permute-done.14.refs_5_
  128.5 0.3 collective-permute-done.15.refs_7_
  128.8 0.8 shard_map.63
  (9 shorter events, 0.1 us)
Async XLA Ops:
  5.2 56.0 %copy-start.5 = (f32[3,2,128,128]{3,2,1,0:T(8,128)S(1)}, f32[3,2,128,128]{3,2,1,0:T(8,128)}, u32[]{:S(2)}) copy-start(f32[3,2,128,128]{3,2,1,0:T(8,128)} %gates_ref.5) | copy-start | bytes 1179652
  61.2 4.1 %copy-start.1 = (f32[32,128,128]{2,1,0:T(8,128)}, f32[32,128,128]{2,1,0:T(8,128)S(1)}, u32[]{:S(2)}) copy-start(f32[32,128,128]{2,1,0:T(8,128)S(1)} %all_to_all.10) | copy-start | bytes 6291460
  65.3 3.7 %copy-start.3 = (f32[2,131072]{1,0:T(2,128)S(1)}, f32[2,131072]{1,0:T(2,128)}, u32[]{:S(2)}) copy-start(f32[2,131072]{1,0:T(2,128)} %param.3) | copy-start | bytes 3145732
  65.4 54.6 %all-to-all-start.1 = ((f32[32,128,128]{2,1,0:T(8,128)}), f32[32,128,128]{2,1,0:T(8,128)S(1)}, u32[]{:S(2)}, u32[]{:S(2)}) async-start(f32[32,128,128]{2,1,0:T(8,128)} %shard_map.59.last_ref), calls=%async_computation.1 | async-start | bytes 4194304 | tf_op jit(solution)/shard_map/all_to_all | solution.py:409
  69.1 1.2 copy-start.4
  70.3 2.4 %copy-start = (f32[32,128,128]{2,1,0:T(8,128)S(1)}, f32[32,128,128]{2,1,0:T(8,128)}, u32[]{:S(2)}) copy-start(f32[32,128,128]{2,1,0:T(8,128)} %shard_map.59.last_ref) | copy-start | bytes 6291460
  72.7 1.6 %copy-start.2 = (f32[32,128,128]{2,1,0:T(8,128)S(1)}, f32[32,128,128]{2,1,0:T(8,128)}, u32[]{:S(2)}) copy-start(f32[32,128,128]{2,1,0:T(8,128)} %copy-done.1) | copy-start | bytes 6291460
  80.2 4.7 %collective-permute-start = (f32[96,128]{1,0:T(8,128)S(1)}, f32[96,128]{1,0:T(8,128)S(1)}, u32[]{:S(2)}, u32[]{:S(2)}) collective-permute-start(f32[96,128]{1,0:T(8,128)S(1)} %get-tuple-element.35), channel_id=1, source_target_pairs={{0,1},{1,0},{2,3},{3,2},{4,5},{5,4},{6,7},{7,6},{8,9},{9,8},{10,11... | collective-permute-start | bytes 147464 | tf_op jit(solution)/shard_map/ppermute | solution.py:298
  80.5 6.1 %collective-permute-start.5 = (f32[96,128]{1,0:T(8,128)S(1)}, f32[96,128]{1,0:T(8,128)S(1)}, u32[]{:S(2)}, u32[]{:S(2)}) collective-permute-start(f32[96,128]{1,0:T(8,128)S(1)} %get-tuple-element.31), channel_id=1, source_target_pairs={{0,6},{1,7},{2,4},{3,5},{4,2},{5,3},{6,0},{7,1},{8,14},{9,15},{10,... | collective-permute-start | bytes 147464 | tf_op jit(solution)/shard_map/ppermute | solution.py:298
  83.1 5.5 %collective-permute-start.6 = (f32[96,128]{1,0:T(8,128)S(1)}, f32[96,128]{1,0:T(8,128)S(1)}, u32[]{:S(2)}, u32[]{:S(2)}) collective-permute-start(f32[96,128]{1,0:T(8,128)S(1)} %get-tuple-element.30), channel_id=1, source_target_pairs={{0,7},{1,6},{2,5},{3,4},{4,3},{5,2},{6,1},{7,0},{8,15},{9,14},{10,... | collective-permute-start | bytes 147464 | tf_op jit(solution)/shard_map/ppermute | solution.py:298
  83.1 8.7 %collective-permute-start.3 = (f32[96,128]{1,0:T(8,128)S(1)}, f32[96,128]{1,0:T(8,128)S(1)}, u32[]{:S(2)}, u32[]{:S(2)}) collective-permute-start(f32[96,128]{1,0:T(8,128)S(1)} %get-tuple-element.33), channel_id=1, source_target_pairs={{0,4},{1,5},{2,6},{3,7},{4,0},{5,1},{6,2},{7,3},{8,12},{9,13},{10,... | collective-permute-start | bytes 147464 | tf_op jit(solution)/shard_map/ppermute | solution.py:298
  84.8 8.7 %collective-permute-start.4 = (f32[96,128]{1,0:T(8,128)S(1)}, f32[96,128]{1,0:T(8,128)S(1)}, u32[]{:S(2)}, u32[]{:S(2)}) collective-permute-start(f32[96,128]{1,0:T(8,128)S(1)} %get-tuple-element.32), channel_id=1, source_target_pairs={{0,5},{1,4},{2,7},{3,6},{4,1},{5,0},{6,3},{7,2},{8,13},{9,12},{10,... | collective-permute-start | bytes 147464 | tf_op jit(solution)/shard_map/ppermute | solution.py:298
  84.9 8.6 %collective-permute-start.1 = (f32[96,128]{1,0:T(8,128)S(1)}, f32[96,128]{1,0:T(8,128)S(1)}, u32[]{:S(2)}, u32[]{:S(2)}) collective-permute-start(f32[96,128]{1,0:T(8,128)S(1)} %get-tuple-element.34), channel_id=1, source_target_pairs={{0,2},{1,3},{2,0},{3,1},{4,6},{5,7},{6,4},{7,5},{8,10},{9,11},{10,... | collective-permute-start | bytes 147464 | tf_op jit(solution)/shard_map/ppermute | solution.py:298
  86.6 6.9 %collective-permute-start.2 = (f32[96,128]{1,0:T(8,128)S(1)}, f32[96,128]{1,0:T(8,128)S(1)}, u32[]{:S(2)}, u32[]{:S(2)}) collective-permute-start(f32[96,128]{1,0:T(8,128)S(1)} %get-tuple-element.29), channel_id=1, source_target_pairs={{0,3},{1,2},{2,1},{3,0},{4,7},{5,6},{6,5},{7,4},{8,11},{9,10},{10,... | collective-permute-start | bytes 147464 | tf_op jit(solution)/shard_map/ppermute | solution.py:298
  93.5 11.7 %collective-permute-start.7 = (f32[96,128]{1,0:T(8,128)S(1)}, f32[96,128]{1,0:T(8,128)S(1)}, u32[]{:S(2)}, u32[]{:S(2)}) collective-permute-start(f32[96,128]{1,0:T(8,128)S(1)} %fusion.1), channel_id=1, source_target_pairs={{0,8},{1,9},{2,10},{3,11},{4,12},{5,13},{6,14},{7,15},{8,0},{9,1},... | collective-permute-start | bytes 147464 | tf_op jit(solution)/shard_map/ppermute | solution.py:298
  105.3 14.7 %collective-permute-start.8 = (f32[96,128]{1,0:T(8,128)S(1)}, f32[96,128]{1,0:T(8,128)S(1)}, u32[]{:S(2)}, u32[]{:S(2)}) collective-permute-start(f32[96,128]{1,0:T(8,128)S(1)} %add.72), channel_id=1, source_target_pairs={{0,16},{1,17},{2,18},{3,19},{4,20},{5,21},{6,22},{7,23},{8,24},{9,... | collective-permute-start | bytes 147464 | tf_op jit(solution)/shard_map/ppermute | solution.py:298
  120.0 7.1 %collective-permute-start.9 = (f32[96,128]{1,0:T(8,128)S(1)}, f32[96,128]{1,0:T(8,128)S(1)}, u32[]{:S(2)}, u32[]{:S(2)}) collective-permute-start(f32[96,128]{1,0:T(8,128)S(1)} %add.73.refs_0_), channel_id=1, source_target_pairs={{0,6},{1,7},{2,4},{3,5},{4,2},{5,3},{6,0},{7,1},{8,14},{9,15},{10,... | collective-permute-start | bytes 147464 | tf_op jit(solution)/shard_map/ppermute | solution.py:298
  122.3 4.7 %collective-permute-start.10 = (f32[96,128]{1,0:T(8,128)S(1)}, f32[96,128]{1,0:T(8,128)S(1)}, u32[]{:S(2)}, u32[]{:S(2)}) collective-permute-start(f32[96,128]{1,0:T(8,128)S(1)} %add.73.refs_0_), channel_id=1, source_target_pairs={{0,4},{1,5},{2,6},{3,7},{4,0},{5,1},{6,2},{7,3},{8,12},{9,13},{10,... | collective-permute-start | bytes 147464 | tf_op jit(solution)/shard_map/ppermute | solution.py:298
  123.0 4.1 %collective-permute-start.11 = (f32[96,128]{1,0:T(8,128)S(1)}, f32[96,128]{1,0:T(8,128)S(1)}, u32[]{:S(2)}, u32[]{:S(2)}) collective-permute-start(f32[96,128]{1,0:T(8,128)S(1)} %add.73.refs_0_), channel_id=1, source_target_pairs={{0,2},{1,3},{2,0},{3,1},{4,6},{5,7},{6,4},{7,5},{8,10},{9,11},{10,... | collective-permute-start | bytes 147464 | tf_op jit(solution)/shard_map/ppermute | solution.py:298
  123.5 4.1 %collective-permute-start.12 = (f32[96,128]{1,0:T(8,128)S(1)}, f32[96,128]{1,0:T(8,128)S(1)}, u32[]{:S(2)}, u32[]{:S(2)}) collective-permute-start(f32[96,128]{1,0:T(8,128)S(1)} %add.73.refs_0_), channel_id=1, source_target_pairs={{0,1},{1,0},{2,3},{3,2},{4,5},{5,4},{6,7},{7,6},{8,9},{9,8},{10,11... | collective-permute-start | bytes 147464 | tf_op jit(solution)/shard_map/ppermute | solution.py:298
  127.1 1.2 collective-permute-start.13
  127.1 1.4 %collective-permute-start.14 = (f32[96,128]{1,0:T(8,128)S(1)}, f32[96,128]{1,0:T(8,128)S(1)}, u32[]{:S(2)}, u32[]{:S(2)}) collective-permute-start(f32[96,128]{1,0:T(8,128)S(1)} %collective-permute-done.10.refs_4_), channel_id=1, source_target_pairs={{0,1},{1,0},{2,3},{3,2},{4,5},{5,4},{6,7},{7,6},{8,9},{9,8},{10,11... | collective-permute-start | bytes 147464 | tf_op jit(solution)/shard_map/ppermute | solution.py:298
  127.6 1.2 collective-permute-start.15
where the time goes:
time: 130 us
  blocking collectives  56 us (43%)
  waiting for transfers between devices  31.2 us (24%)
  Pallas kernels  20 us (15%)
  starting transfers between devices  18.7 us (14%)
  local copies, waits for them, and re-layouts  2.87 us (2%)
    all_to_all x1, blocking collectives, on_device_lanes(): moved = lax.all_to_all(sent, 'amp', 0, 0, tiled=True)  56 us
    ppermute x16, waiting for transfers between devices, exchange(): lax.ppermute(part, 'amp', [(i, i ^ distance) for i in range(devices)])  31.2 us
    ppermute x16, starting transfers between devices, exchange(): lax.ppermute(part, 'amp', [(i, i ^ distance) for i in range(devices)])  15 us
    pallas_call x1, Pallas kernels, on_device_lanes(): pl.pallas_call(functools.partial(late_kernel, scale=scale), in_specs=[IN_...  5.82 us
    pallas_call x1, Pallas kernels, on_device_lanes(): pl.pallas_call(first_kernel, in_specs=[IN_HBM, IN_HBM, IN_HBM], out_specs...  4.51 us
    pallas_call x1, Pallas kernels, on_device_lanes(): pl.pallas_call(middle_kernel, in_specs=[IN_VMEM, IN_VMEM], out_specs=IN_H...  4.13 us
    all_to_all x1, starting transfers between devices, on_device_lanes(): arrived = lax.all_to_all(last, 'amp', 0, 0, tiled=True)  3.67 us
    unnamed x12, local copies, waits for them, and re-layouts  2.82 us
  transfers between devices with their start and end apart: 17, of which 9 were waited for; matrix products, arithmetic and copies ran while one was open for 0% of the time, Pallas kernels for 8%

commit v1 on v0

--- a/solution.py
+++ b/solution.py
@@ -194,9 +194,9 @@
         fields = [regrouped(kept, step * 2 + index, order) for index in range(2)]
         for index, result in enumerate(undo(matrices[1], fields)):
             for bit, piece in enumerate(swap_bit(*row_halves(result, 2))):
-                last[bit * batches + step * 2 + index] = piece
+                last[2 * batches - 1 - (bit * batches + step * 2 + index)] = piece
         for bit in range(2):
-            part = pl.ds(bit * batches + step * 2, 2)
+            part = pl.ds(2 * batches - 2 - (bit * batches + step * 2), 2)
             copy = pltpu.make_async_copy(last.at[part], out_ref.at[part], sems.at[bit, step])
             copy.start()
             copies.append(copy)
@@ -213,8 +213,9 @@
 
 def mixed_rows(moved_ref, step, bit):
     low_rows = moved_ref.shape[3] // 4
+    last_step = moved_ref.shape[1] - 1
     parts = [
-        moved_ref[top, step, low, pl.ds((part * 2 + bit) * low_rows, low_rows), :]
+        moved_ref[1 - top, last_step - step, 1 - low, pl.ds((part * 2 + bit) * low_rows, low_rows), :]
         for part in range(2)
         for top in range(2)
         for low in range(2)
@@ -291,6 +292,11 @@
     while len(parts) > 1:
         parts = [parts[i] + parts[i + 1] for i in range(0, len(parts), 2)]
     return parts[0]
+
+
+def exchange_all(field):
+    group = list(reversed(range(lax.axis_size("amp"))))
+    return lax.all_to_all(field, "amp", 0, 0, axis_index_groups=[group], tiled=True)
 
 
 def exchange(part, distance):
@@ -383,7 +389,7 @@
         cost_estimate=cost(1, amplitudes, order),
     )(state, costate, gates)
     state, costate, sent = lax.optimization_barrier((state, costate, sent))
-    moved = lax.all_to_all(sent, "amp", 0, 0, tiled=True)
+    moved = exchange_all(sent)
     early = pl.pallas_call(
         early_kernel,
         in_specs=[IN_VMEM, IN_VMEM],
@@ -406,7 +412,7 @@
         compiler_params=PARAMS,
         cost_estimate=cost(2, amplitudes, order),
     )(moved, gates)
-    arrived = lax.all_to_all(last, "amp", 0, 0, tiled=True)
+    arrived = exchange_all(last)
     gradients = pl.pallas_call(
         functools.partial(late_kernel, scale=scale),
         in_specs=[IN_VMEM, IN_VMEM, IN_VMEM, IN_VMEM],

time: 130 us -> 130 us (level)
  starting transfers between devices: 18.7 us -> 25.6 us
  waiting for transfers between devices: 31.2 us -> 24.4 us
    ppermute x16, starting transfers between devices: 15 us -> 22 us  [exchange(): lax.ppermute(part, 'amp', [(i, i ^ distance) for i in range(devices)])]
    ppermute x16, waiting for transfers between devices: 31.2 us -> 24.4 us  [exchange(): lax.ppermute(part, 'amp', [(i, i ^ distance) for i in range(devices)])]
where the time goes in v1:
time: 130 us
  blocking collectives  56 us (43%)
  starting transfers between devices  25.6 us (20%)
  waiting for transfers between devices  24.4 us (19%)
  Pallas kernels  20 us (15%)
  local copies, waits for them, and re-layouts  2.87 us (2%)
    all_to_all x1, blocking collectives, exchange_all(): lax.all_to_all(field, 'amp', 0, 0, axis_index_groups=[group], tiled=True)  56 us
    ppermute x16, waiting for transfers between devices, exchange(): lax.ppermute(part, 'amp', [(i, i ^ distance) for i in range(devices)])  24.4 us
    ppermute x16, starting transfers between devices, exchange(): lax.ppermute(part, 'amp', [(i, i ^ distance) for i in range(devices)])  22 us
    pallas_call x1, Pallas kernels, on_device_lanes(): pl.pallas_call(functools.partial(late_kernel, scale=scale), in_specs=[IN_...  5.82 us
    pallas_call x1, Pallas kernels, on_device_lanes(): pl.pallas_call(first_kernel, in_specs=[IN_HBM, IN_HBM, IN_HBM], out_specs...  4.51 us
    pallas_call x1, Pallas kernels, on_device_lanes(): pl.pallas_call(middle_kernel, in_specs=[IN_VMEM, IN_VMEM], out_specs=IN_H...  4.13 us
    all_to_all x1, starting transfers between devices, exchange_all(): lax.all_to_all(field, 'amp', 0, 0, axis_index_groups=[group], tiled=True)  3.62 us
    unnamed x12, local copies, waits for them, and re-layouts  2.82 us
  transfers between devices with their start and end apart: 17, of which 9 were waited for; matrix products, arithmetic and copies ran while one was open for 0% of the time, Pallas kernels for 8%

profile of v1, /device:TPU:0, one launch (start us, length us, event | category | flops | bytes accessed | tf_op | source)
XLA Modules:
  0.0 129.8 jit_solution(12563628598053393965)
XLA Ops:
  0.6 4.5 %shard_map.58 = f32[32,128,128]{2,1,0:T(8,128)} custom-call(f32[2048,128]{1,0:T(8,128)} %bitcast.45, f32[2048,128]{1,0:T(8,128)} %bitcast.47, f32[3,2,128,128]{3,2,1,0:T(8,128)} %gates_ref.5), custom_call_target="tpu_custom_call" | custom-call | flops 805306368 | bytes 8388608 | tf_op jit(solution)/shard_map/pallas_call | solution.py:375
  5.2 0.0 copy-start.5
  5.2 56.0 %all_to_all.10 = f32[32,128,128]{2,1,0:T(8,128)S(1)} all-to-all(f32[32,128,128]{2,1,0:T(8,128)} %shard_map.58), channel_id=1, replica_groups={{31,30,29,28,27,26,25,24,23,22,21,20,19,18,17,16,15,14,13,12,11,10,9,8,..., dimensions={0} | all-to-all | bytes 4194304 | tf_op jit(solution)/shard_map/all_to_all | solution.py:299
  61.2 0.0 copy-done.5
  61.2 4.1 %shard_map.59.last_ref = f32[32,128,128]{2,1,0:T(8,128)} custom-call(f32[2,8,2,128,128]{4,3,2,1,0:T(8,128)S(1)} %bitcast.43, f32[3,2,128,128]{3,2,1,0:T(8,128)S(1)} %copy-done.5), custom_call_target="tpu_custom_call" | custom-call | flops 1610612736 | bytes 8388608 | tf_op jit(solution)/shard_map/pallas_call | solution.py:402
  65.3 0.0 copy-start.3
  65.4 3.6 %all-to-all-start.1 = ((f32[32,128,128]{2,1,0:T(8,128)}), f32[32,128,128]{2,1,0:T(8,128)S(1)}, u32[]{:S(2)}, u32[]{:S(2)}) async-start(f32[32,128,128]{2,1,0:T(8,128)} %shard_map.59.last_ref), calls=%async_computation.1 | async-start | bytes 4194304 | tf_op jit(solution)/shard_map/all_to_all | solution.py:299
  69.0 0.0 copy-done.3
  69.0 0.0 copy-start.4
  69.1 1.2 copy-done.4
  70.3 2.4 %shard_map.60.early_ref = f32[128,256]{1,0:T(8,128)S(1)} custom-call(f32[2048,128]{1,0:T(8,128)S(1)} %bitcast.46, f32[2048,128]{1,0:T(8,128)S(1)} %bitcast.48), custom_call_target="tpu_custom_call" | custom-call | flops 805306368 | bytes 8388608 | tf_op jit(solution)/shard_map/pallas_call | solution.py:393
  72.7 1.6 %copy-done.2 = f32[32,128,128]{2,1,0:T(8,128)S(1)} copy-done((f32[32,128,128]{2,1,0:T(8,128)S(1)}, f32[32,128,128]{2,1,0:T(8,128)}, u32[]{:S(2)}) %copy-start.2) | copy-done | bytes 2097176
  74.2 5.8 %shard_map.61 = f32[3,2,128,128]{3,2,1,0:T(8,128)S(1)} custom-call(f32[2,8,2,128,128]{4,3,2,1,0:T(8,128)S(1)} %bitcast.44, f32[32,128,128]{2,1,0:T(8,128)S(1)} %copy-done, f32[128,256]{1,0:T(8,128)S(1)} %shard_map.60.early_ref, f32[3,2,128,128]{3,2,1,0:T(8,128)S(1)} %copy-done.5), custom_call_target="tpu_custom_call" | custom-call | flops 1610612736 | bytes 8388608 | tf_op jit(solution)/shard_map/pallas_call | solution.py:416
  80.1 0.4 collective-permute-start
  80.5 2.5 %collective-permute-start.5 = (f32[96,128]{1,0:T(8,128)S(1)}, f32[96,128]{1,0:T(8,128)S(1)}, u32[]{:S(2)}, u32[]{:S(2)}) collective-permute-start(f32[96,128]{1,0:T(8,128)S(1)} %get-tuple-element.31), channel_id=1, source_target_pairs={{0,6},{1,7},{2,4},{3,5},{4,2},{5,3},{6,0},{7,1},{8,14},{9,15},{10,... | collective-permute-start | bytes 147464 | tf_op jit(solution)/shard_map/ppermute | solution.py:304
  83.0 0.0 collective-permute-start.6
  83.0 1.7 %collective-permute-start.3 = (f32[96,128]{1,0:T(8,128)S(1)}, f32[96,128]{1,0:T(8,128)S(1)}, u32[]{:S(2)}, u32[]{:S(2)}) collective-permute-start(f32[96,128]{1,0:T(8,128)S(1)} %get-tuple-element.33), channel_id=1, source_target_pairs={{0,4},{1,5},{2,6},{3,7},{4,0},{5,1},{6,2},{7,3},{8,12},{9,13},{10,... | collective-permute-start | bytes 147464 | tf_op jit(solution)/shard_map/ppermute | solution.py:304
  84.7 0.2 collective-permute-start.4
  84.9 0.0 collective-permute-done
  84.9 1.6 %collective-permute-start.1 = (f32[96,128]{1,0:T(8,128)S(1)}, f32[96,128]{1,0:T(8,128)S(1)}, u32[]{:S(2)}, u32[]{:S(2)}) collective-permute-start(f32[96,128]{1,0:T(8,128)S(1)} %get-tuple-element.34), channel_id=1, source_target_pairs={{0,2},{1,3},{2,0},{3,1},{4,6},{5,7},{6,4},{7,5},{8,10},{9,11},{10,... | collective-permute-start | bytes 147464 | tf_op jit(solution)/shard_map/ppermute | solution.py:304
  86.5 0.0 collective-permute-done.5
  86.5 3.7 %collective-permute-start.2 = (f32[96,128]{1,0:T(8,128)S(1)}, f32[96,128]{1,0:T(8,128)S(1)}, u32[]{:S(2)}, u32[]{:S(2)}) collective-permute-start(f32[96,128]{1,0:T(8,128)S(1)} %get-tuple-element.29), channel_id=1, source_target_pairs={{0,3},{1,2},{2,1},{3,0},{4,7},{5,6},{6,5},{7,4},{8,11},{9,10},{10,... | collective-permute-start | bytes 147464 | tf_op jit(solution)/shard_map/ppermute | solution.py:304
  90.2 1.9 %collective-permute-done.6 = f32[96,128]{1,0:T(8,128)S(1)} collective-permute-done((f32[96,128]{1,0:T(8,128)S(1)}, f32[96,128]{1,0:T(8,128)S(1)}, u32[]{:S(2)}, u32[]{:S(2)}) %collective-permute-start.6) | collective-permute-done | bytes 49184 | tf_op jit(solution)/shard_map/ppermute | solution.py:304
  92.1 0.0 collective-permute-done.3
  92.1 0.9 collective-permute-done.4
  92.9 0.0 collective-permute-done.1
  92.9 0.6 collective-permute-done.2
  93.5 3.6 %collective-permute-start.7 = (f32[96,128]{1,0:T(8,128)S(1)}, f32[96,128]{1,0:T(8,128)S(1)}, u32[]{:S(2)}, u32[]{:S(2)}) collective-permute-start(f32[96,128]{1,0:T(8,128)S(1)} %fusion.1), channel_id=1, source_target_pairs={{0,8},{1,9},{2,10},{3,11},{4,12},{5,13},{6,14},{7,15},{8,0},{9,1},... | collective-permute-start | bytes 147464 | tf_op jit(solution)/shard_map/ppermute | solution.py:304
  97.1 7.9 %collective-permute-done.7 = f32[96,128]{1,0:T(8,128)S(1)} collective-permute-done((f32[96,128]{1,0:T(8,128)S(1)}, f32[96,128]{1,0:T(8,128)S(1)}, u32[]{:S(2)}, u32[]{:S(2)}) %collective-permute-start.7) | collective-permute-done | bytes 49184 | tf_op jit(solution)/shard_map/ppermute | solution.py:304
  105.0 4.3 %collective-permute-start.8 = (f32[96,128]{1,0:T(8,128)S(1)}, f32[96,128]{1,0:T(8,128)S(1)}, u32[]{:S(2)}, u32[]{:S(2)}) collective-permute-start(f32[96,128]{1,0:T(8,128)S(1)} %add.72), channel_id=1, source_target_pairs={{0,16},{1,17},{2,18},{3,19},{4,20},{5,21},{6,22},{7,23},{8,24},{9,... | collective-permute-start | bytes 147464 | tf_op jit(solution)/shard_map/ppermute | solution.py:304
  109.3 10.5 %collective-permute-done.8 = f32[96,128]{1,0:T(8,128)S(1)} collective-permute-done((f32[96,128]{1,0:T(8,128)S(1)}, f32[96,128]{1,0:T(8,128)S(1)}, u32[]{:S(2)}, u32[]{:S(2)}) %collective-permute-start.8) | collective-permute-done | bytes 49184 | tf_op jit(solution)/shard_map/ppermute | solution.py:304
  119.8 0.0 all-to-all-done.1.moved_ref
  119.8 2.5 %collective-permute-start.9 = (f32[96,128]{1,0:T(8,128)S(1)}, f32[96,128]{1,0:T(8,128)S(1)}, u32[]{:S(2)}, u32[]{:S(2)}) collective-permute-start(f32[96,128]{1,0:T(8,128)S(1)} %add.73.refs_0_), channel_id=1, source_target_pairs={{0,6},{1,7},{2,4},{3,5},{4,2},{5,3},{6,0},{7,1},{8,14},{9,15},{10,... | collective-permute-start | bytes 147464 | tf_op jit(solution)/shard_map/ppermute | solution.py:304
  122.3 0.8 collective-permute-start.10
  123.1 0.3 collective-permute-start.11
  123.4 0.0 collective-permute-start.12
  123.4 2.4 %shard_map.62 = (f32[128,16,1,128]{3,2,1,0:T(1,128)}, f32[128,16,1,128]{3,2,1,0:T(1,128)}) custom-call(f32[32,128,128]{2,1,0:T(8,128)S(1)} %all-to-all-done.1.moved_ref), custom_call_target="tpu_custom_call" | custom-call | flops 805306368 | bytes 8388608 | tf_op jit(solution)/shard_map/pallas_call | solution.py:427
  125.8 1.4 %collective-permute-done.11.refs_2_ = f32[96,128]{1,0:T(8,128)S(1)} collective-permute-done((f32[96,128]{1,0:T(8,128)S(1)}, f32[96,128]{1,0:T(8,128)S(1)}, u32[]{:S(2)}, u32[]{:S(2)}) %collective-permute-start.11) | collective-permute-done | bytes 49184 | tf_op jit(solution)/shard_map/ppermute | solution.py:304
  127.2 0.0 collective-permute-done.10.refs_4_
  127.2 0.0 collective-permute-done.9.refs_6_
  127.2 0.0 collective-permute-start.13
  127.2 0.5 collective-permute-start.14
  127.7 0.1 collective-permute-start.15
  127.8 0.0 collective-permute-done.12.refs_1_
  127.8 0.6 collective-permute-done.13.refs_3_
  128.4 0.2 collective-permute-done.14.refs_5_
  128.6 0.3 collective-permute-done.15.refs_7_
  129.0 0.8 shard_map.63
  (9 shorter events, 0.1 us)
Async XLA Ops:
  5.2 56.0 %copy-start.5 = (f32[3,2,128,128]{3,2,1,0:T(8,128)S(1)}, f32[3,2,128,128]{3,2,1,0:T(8,128)}, u32[]{:S(2)}) copy-start(f32[3,2,128,128]{3,2,1,0:T(8,128)} %gates_ref.5) | copy-start | bytes 1179652
  61.2 4.1 %copy-start.1 = (f32[32,128,128]{2,1,0:T(8,128)}, f32[32,128,128]{2,1,0:T(8,128)S(1)}, u32[]{:S(2)}) copy-start(f32[32,128,128]{2,1,0:T(8,128)S(1)} %all_to_all.10) | copy-start | bytes 6291460
  65.3 3.7 %copy-start.3 = (f32[2,131072]{1,0:T(2,128)S(1)}, f32[2,131072]{1,0:T(2,128)}, u32[]{:S(2)}) copy-start(f32[2,131072]{1,0:T(2,128)} %param.3) | copy-start | bytes 3145732
  65.4 54.5 %all-to-all-start.1 = ((f32[32,128,128]{2,1,0:T(8,128)}), f32[32,128,128]{2,1,0:T(8,128)S(1)}, u32[]{:S(2)}, u32[]{:S(2)}) async-start(f32[32,128,128]{2,1,0:T(8,128)} %shard_map.59.last_ref), calls=%async_computation.1 | async-start | bytes 4194304 | tf_op jit(solution)/shard_map/all_to_all | solution.py:299
  69.0 1.2 copy-start.4
  70.3 2.4 %copy-start = (f32[32,128,128]{2,1,0:T(8,128)S(1)}, f32[32,128,128]{2,1,0:T(8,128)}, u32[]{:S(2)}) copy-start(f32[32,128,128]{2,1,0:T(8,128)} %shard_map.59.last_ref) | copy-start | bytes 6291460
  72.7 1.6 %copy-start.2 = (f32[32,128,128]{2,1,0:T(8,128)S(1)}, f32[32,128,128]{2,1,0:T(8,128)}, u32[]{:S(2)}) copy-start(f32[32,128,128]{2,1,0:T(8,128)} %copy-done.1) | copy-start | bytes 6291460
  80.1 4.8 %collective-permute-start = (f32[96,128]{1,0:T(8,128)S(1)}, f32[96,128]{1,0:T(8,128)S(1)}, u32[]{:S(2)}, u32[]{:S(2)}) collective-permute-start(f32[96,128]{1,0:T(8,128)S(1)} %get-tuple-element.35), channel_id=1, source_target_pairs={{0,1},{1,0},{2,3},{3,2},{4,5},{5,4},{6,7},{7,6},{8,9},{9,8},{10,11... | collective-permute-start | bytes 147464 | tf_op jit(solution)/shard_map/ppermute | solution.py:304
  80.5 6.0 %collective-permute-start.5 = (f32[96,128]{1,0:T(8,128)S(1)}, f32[96,128]{1,0:T(8,128)S(1)}, u32[]{:S(2)}, u32[]{:S(2)}) collective-permute-start(f32[96,128]{1,0:T(8,128)S(1)} %get-tuple-element.31), channel_id=1, source_target_pairs={{0,6},{1,7},{2,4},{3,5},{4,2},{5,3},{6,0},{7,1},{8,14},{9,15},{10,... | collective-permute-start | bytes 147464 | tf_op jit(solution)/shard_map/ppermute | solution.py:304
  83.0 9.0 %collective-permute-start.6 = (f32[96,128]{1,0:T(8,128)S(1)}, f32[96,128]{1,0:T(8,128)S(1)}, u32[]{:S(2)}, u32[]{:S(2)}) collective-permute-start(f32[96,128]{1,0:T(8,128)S(1)} %get-tuple-element.30), channel_id=1, source_target_pairs={{0,7},{1,6},{2,5},{3,4},{4,3},{5,2},{6,1},{7,0},{8,15},{9,14},{10,... | collective-permute-start | bytes 147464 | tf_op jit(solution)/shard_map/ppermute | solution.py:304
  83.0 9.0 %collective-permute-start.3 = (f32[96,128]{1,0:T(8,128)S(1)}, f32[96,128]{1,0:T(8,128)S(1)}, u32[]{:S(2)}, u32[]{:S(2)}) collective-permute-start(f32[96,128]{1,0:T(8,128)S(1)} %get-tuple-element.33), channel_id=1, source_target_pairs={{0,4},{1,5},{2,6},{3,7},{4,0},{5,1},{6,2},{7,3},{8,12},{9,13},{10,... | collective-permute-start | bytes 147464 | tf_op jit(solution)/shard_map/ppermute | solution.py:304
  84.7 8.2 %collective-permute-start.4 = (f32[96,128]{1,0:T(8,128)S(1)}, f32[96,128]{1,0:T(8,128)S(1)}, u32[]{:S(2)}, u32[]{:S(2)}) collective-permute-start(f32[96,128]{1,0:T(8,128)S(1)} %get-tuple-element.32), channel_id=1, source_target_pairs={{0,5},{1,4},{2,7},{3,6},{4,1},{5,0},{6,3},{7,2},{8,13},{9,12},{10,... | collective-permute-start | bytes 147464 | tf_op jit(solution)/shard_map/ppermute | solution.py:304
  84.9 8.0 %collective-permute-start.1 = (f32[96,128]{1,0:T(8,128)S(1)}, f32[96,128]{1,0:T(8,128)S(1)}, u32[]{:S(2)}, u32[]{:S(2)}) collective-permute-start(f32[96,128]{1,0:T(8,128)S(1)} %get-tuple-element.34), channel_id=1, source_target_pairs={{0,2},{1,3},{2,0},{3,1},{4,6},{5,7},{6,4},{7,5},{8,10},{9,11},{10,... | collective-permute-start | bytes 147464 | tf_op jit(solution)/shard_map/ppermute | solution.py:304
  86.5 7.0 %collective-permute-start.2 = (f32[96,128]{1,0:T(8,128)S(1)}, f32[96,128]{1,0:T(8,128)S(1)}, u32[]{:S(2)}, u32[]{:S(2)}) collective-permute-start(f32[96,128]{1,0:T(8,128)S(1)} %get-tuple-element.29), channel_id=1, source_target_pairs={{0,3},{1,2},{2,1},{3,0},{4,7},{5,6},{6,5},{7,4},{8,11},{9,10},{10,... | collective-permute-start | bytes 147464 | tf_op jit(solution)/shard_map/ppermute | solution.py:304
  93.5 11.5 %collective-permute-start.7 = (f32[96,128]{1,0:T(8,128)S(1)}, f32[96,128]{1,0:T(8,128)S(1)}, u32[]{:S(2)}, u32[]{:S(2)}) collective-permute-start(f32[96,128]{1,0:T(8,128)S(1)} %fusion.1), channel_id=1, source_target_pairs={{0,8},{1,9},{2,10},{3,11},{4,12},{5,13},{6,14},{7,15},{8,0},{9,1},... | collective-permute-start | bytes 147464 | tf_op jit(solution)/shard_map/ppermute | solution.py:304
  105.0 14.8 %collective-permute-start.8 = (f32[96,128]{1,0:T(8,128)S(1)}, f32[96,128]{1,0:T(8,128)S(1)}, u32[]{:S(2)}, u32[]{:S(2)}) collective-permute-start(f32[96,128]{1,0:T(8,128)S(1)} %add.72), channel_id=1, source_target_pairs={{0,16},{1,17},{2,18},{3,19},{4,20},{5,21},{6,22},{7,23},{8,24},{9,... | collective-permute-start | bytes 147464 | tf_op jit(solution)/shard_map/ppermute | solution.py:304
  119.8 7.4 %collective-permute-start.9 = (f32[96,128]{1,0:T(8,128)S(1)}, f32[96,128]{1,0:T(8,128)S(1)}, u32[]{:S(2)}, u32[]{:S(2)}) collective-permute-start(f32[96,128]{1,0:T(8,128)S(1)} %add.73.refs_0_), channel_id=1, source_target_pairs={{0,6},{1,7},{2,4},{3,5},{4,2},{5,3},{6,0},{7,1},{8,14},{9,15},{10,... | collective-permute-start | bytes 147464 | tf_op jit(solution)/shard_map/ppermute | solution.py:304
  122.3 4.9 %collective-permute-start.10 = (f32[96,128]{1,0:T(8,128)S(1)}, f32[96,128]{1,0:T(8,128)S(1)}, u32[]{:S(2)}, u32[]{:S(2)}) collective-permute-start(f32[96,128]{1,0:T(8,128)S(1)} %add.73.refs_0_), channel_id=1, source_target_pairs={{0,4},{1,5},{2,6},{3,7},{4,0},{5,1},{6,2},{7,3},{8,12},{9,13},{10,... | collective-permute-start | bytes 147464 | tf_op jit(solution)/shard_map/ppermute | solution.py:304
  123.1 4.1 %collective-permute-start.11 = (f32[96,128]{1,0:T(8,128)S(1)}, f32[96,128]{1,0:T(8,128)S(1)}, u32[]{:S(2)}, u32[]{:S(2)}) collective-permute-start(f32[96,128]{1,0:T(8,128)S(1)} %add.73.refs_0_), channel_id=1, source_target_pairs={{0,2},{1,3},{2,0},{3,1},{4,6},{5,7},{6,4},{7,5},{8,10},{9,11},{10,... | collective-permute-start | bytes 147464 | tf_op jit(solution)/shard_map/ppermute | solution.py:304
  123.4 4.4 %collective-permute-start.12 = (f32[96,128]{1,0:T(8,128)S(1)}, f32[96,128]{1,0:T(8,128)S(1)}, u32[]{:S(2)}, u32[]{:S(2)}) collective-permute-start(f32[96,128]{1,0:T(8,128)S(1)} %add.73.refs_0_), channel_id=1, source_target_pairs={{0,1},{1,0},{2,3},{3,2},{4,5},{5,4},{6,7},{7,6},{8,9},{9,8},{10,11... | collective-permute-start | bytes 147464 | tf_op jit(solution)/shard_map/ppermute | solution.py:304
  127.2 1.2 collective-permute-start.13
  127.2 1.4 %collective-permute-start.14 = (f32[96,128]{1,0:T(8,128)S(1)}, f32[96,128]{1,0:T(8,128)S(1)}, u32[]{:S(2)}, u32[]{:S(2)}) collective-permute-start(f32[96,128]{1,0:T(8,128)S(1)} %collective-permute-done.10.refs_4_), channel_id=1, source_target_pairs={{0,1},{1,0},{2,3},{3,2},{4,5},{5,4},{6,7},{7,6},{8,9},{9,8},{10,11... | collective-permute-start | bytes 147464 | tf_op jit(solution)/shard_map/ppermute | solution.py:304
  127.7 1.2 collective-permute-start.15
